TPU v7x, 128 devices: a whole 4x4x4 slice. The times are simulated.
128 devices in a mesh: dp: 4 (over z), mp: 32 (over x, y, core).
Axes of the slice: x: 4, y: 4, z: 4, core: 2. Of those that a mesh axis runs over, the one named last changes fastest.
Arguments:
- tokens: bfloat16 [16384, 4096], P(('dp', 'mp')), may hold values from -6 to 6
- expert_ids: int32 [16384, 1], P(('dp', 'mp')), may hold values from 0 to 63; in each aligned block of 128 rows (0 to 127, 128 to 255, ...) at most 3 rows name the same one
- gate_probs: float32 [16384, 1], P(('dp', 'mp')), may hold values from 0.3 to 1
- gate_weight: bfloat16 [64, 4096, 1536], P('mp', None, 'dp'), may hold values from -0.09375 to 0.09375
- up_weight: bfloat16 [64, 4096, 1536], P('mp', None, 'dp'), may hold values from -0.09375 to 0.09375
- down_weight: bfloat16 [64, 1536, 4096], P('mp', 'dp'), may hold values from -0.15625 to 0.15625
- sign_offset: int32 [1], replicated, may hold values from 1 to 999999999
Outputs:
- out_plus: bfloat16 [16384, 4096], P(('dp', 'mp'))
- out_minus: bfloat16 [16384, 4096], P(('dp', 'mp'))
Inputs may be any that keep to these rules, and one draw needn't show every extreme that they name: `expert_ids`: within each aligned block of 128 tokens (the tokens of one device) no expert is named by more than 3 routes, a bound that some block reaches.
All inputs are finite; a program needn't handle non-finite values.
Results may differ from a plain program's by a relative error of at most 0.01.
Values may be sent and summed in bfloat16 or wider, within the bound.
A program may use at most 128 MiB of HBM per device.

v0:
```python
import jax
import jax.numpy as jnp
import numpy as np
from jax import lax
from jax.experimental import pallas as pl
from jax.experimental.pallas import tpu as pltpu
from jax.sharding import PartitionSpec as P

D = 4096
FF = 1536
Q = 384
CAP = 3
ROWS = 96
HALF = 48
MSG = 48
PEERS = 32
EPS = 0.005
MESH = pl.DeviceIdType.MESH
F32, BF16, I32 = jnp.float32, jnp.bfloat16, jnp.int32


def mixing(number):
    number = number ^ lax.shift_right_logical(number, jnp.full_like(number, 16))
    number = number * 73244475
    number = number ^ lax.shift_right_logical(number, jnp.full_like(number, 16))
    number = number * 73244475
    return number ^ lax.shift_right_logical(number, jnp.full_like(number, 16))


def moved_by(position, offset_mixed):
    hashed = mixing(position ^ offset_mixed)
    return jnp.where((hashed & 512) != 0, EPS, -EPS).astype(F32)


def kernel(
    ids_row, ids_col, probs, sign_offset, swap, slots_col, slots_row, tokens, gate_w, up_w, down_w,
    out_plus, out_minus,
    rows, sent, came, wide, down, part, relay, home, back, acc, hidden, perm,
    w_sem, a_send, a_recv, z_send, z_recv, p_send, r_recv, h_recv, b_send, b_recv, o_sem,
):
    z, m = lax.axis_index("dp"), lax.axis_index("mp")
    x, y, core = m // 8, (m // 2) % 4, m % 2
    above, below = (z + 1) % 4, (z + 3) % 4
    hidden_base = z * Q

    def peer(p, sign):
        return (
            (x + sign * (p // 8) + 4) % 4 * 8
            + (y + sign * ((p // 2) % 4) + 4) % 4 * 2
            + (core + p) % 2
        )

    def load_weights(e):
        for i, (source, target) in enumerate(
            (
                (gate_w, wide.at[0, :, 0:Q]),
                (up_w, wide.at[0, :, Q : 2 * Q]),
                (down_w, down.at[0]),
            )
        ):
            yield pltpu.make_async_copy(source.at[e], target, w_sem.at[i])

    for copy in load_weights(0):
        copy.start()

    barrier = pltpu.get_barrier_semaphore()

    @pl.loop(1, PEERS)
    def _(p):
        pl.semaphore_signal(barrier, inc=1, device_id=(z, peer(p, -1)), device_id_type=MESH)

    for near in (above, below):
        pl.semaphore_signal(barrier, inc=1, device_id=(near, m), device_id_type=MESH)
    pl.semaphore_wait(barrier, PEERS + 1)

    alike = ids_col[...] == ids_row[...]
    at_row = lax.broadcasted_iota(I32, (128, 128), 0)
    at_col = lax.broadcasted_iota(I32, (128, 128), 1)
    key_col = ids_col[...] * 4 + jnp.sum(
        jnp.where(alike & (at_col < at_row), 1, 0), axis=1, keepdims=True
    )
    key_row = ids_row[...] * 4 + jnp.sum(
        jnp.where(alike & (at_row < at_col), 1, 0), axis=0, keepdims=True
    )

    def slot_keys(a, b, d, s, e):
        owner = ((x - a) & 3) * 8 + ((y - b) & 3) * 2 + ((core + d) & 1)
        return (owner * 2 + e) * 4 + s

    perm[...] = jnp.where(
        lax.broadcasted_iota(I32, (768, 768), 1) == swap[...], 1.0, 0.0
    ).astype(BF16)

    def pack(source, target, i, half):
        stacked = jnp.concatenate(
            [
                source[half * HALF : (half + 1) * HALF, c * 256 : (c + 1) * 256]
                for c in range(16)
            ],
            axis=0,
        )
        target[i, half * 768 : (half + 1) * 768, :] = jnp.dot(
            perm[...], stacked, preferred_element_type=F32
        ).astype(BF16)

    def unpack(source, i, half, target):
        laid = jnp.dot(
            perm[...], source[i, half * 768 : (half + 1) * 768, :], preferred_element_type=F32
        ).astype(BF16)
        for c in range(16):
            target[half * HALF : (half + 1) * HALF, c * 256 : (c + 1) * 256] = laid[
                c * HALF : (c + 1) * HALF
            ]

    def exchange(i, target, j, sign, half, send_sem, recv_sem):
        @pl.loop(max(1, half * 16), half * 16 + 16)
        def _(p):
            at = pl.ds(pl.multiple_of(p * MSG, MSG), MSG)
            pltpu.make_async_remote_copy(
                sent.at[i, at], target.at[j, at], send_sem, recv_sem,
                device_id=(z, peer(p, sign)), device_id_type=MESH,
            ).start()

    def whole(i, target, j, lo, hi, send_sem, recv_sem):
        return pltpu.make_async_remote_copy(
            sent.at[i, lo:hi], target.at[j, lo:hi], send_sem, recv_sem,
            device_id=(z, peer(1, 1)), device_id_type=MESH,
        )

    for e in range(2):
        chosen = jnp.where(
            key_row == slot_keys(*[slots_col[:, i : i + 1] for i in range(4)], e), 1.0, 0.0
        ).astype(BF16)
        staged = part.at[0, e]
        for c in range(4):
            cols = slice(c * 1024, (c + 1) * 1024)
            staged[0:ROWS, cols] = jnp.dot(
                chosen, tokens[:, cols], preferred_element_type=F32
            ).astype(BF16)
        for half in range(2):
            pack(staged, sent, e, half)
            exchange(e, came, e, -1, half, a_send.at[e], a_recv.at[e, half])
        came[e, 0:MSG, :] = sent[e, 0:MSG, :]

    offset_mixed = mixing(sign_offset[0] * 668265261 + 12345)

    def move_wide(e, lo, hi):
        expert = m * 2 + e
        inner = lax.broadcasted_iota(I32, (32, Q), 0) * (3 * FF) + lax.broadcasted_iota(
            I32, (32, Q), 1
        ) * 3

        @pl.loop(lo, hi)
        def _(i):
            at = pl.ds(pl.multiple_of(i * 32, 32), 32)
            first = ((expert * D + i * 32) * FF + hidden_base) * 3
            for tag in range(2):
                cols = slice(tag * Q, (tag + 1) * Q)
                weight = wide[0, at, cols].astype(F32)
                step = moved_by(inner + (first + tag), offset_mixed)
                wide[0, at, cols] = (weight + step).astype(BF16)
                wide[1, at, cols] = (weight - step).astype(BF16)

    def move_down(e, lo, hi):
        expert = m * 2 + e
        inner = lax.broadcasted_iota(I32, (32, 512), 0) * (3 * D) + lax.broadcasted_iota(
            I32, (32, 512), 1
        ) * 3

        @pl.loop(lo, hi)
        def _(i):
            row, col = i // 8 * 32, i % 8 * 512
            at, cols = pl.ds(pl.multiple_of(row, 32), 32), pl.ds(pl.multiple_of(col, 512), 512)
            first = ((expert * FF + hidden_base + row) * D + col) * 3 + 2
            weight = down[0, at, cols].astype(F32)
            step = moved_by(inner + first, offset_mixed)
            down[0, at, cols] = (weight + step).astype(BF16)
            down[1, at, cols] = (weight - step).astype(BF16)

    def gather_copy(e, from_slot, to_slot, half, n, to):
        return pltpu.make_async_remote_copy(
            rows.at[e, from_slot * ROWS + half * HALF : from_slot * ROWS + (half + 1) * HALF],
            rows.at[e, to_slot * ROWS + half * HALF : to_slot * ROWS + (half + 1) * HALF],
            z_send.at[e, n], z_recv.at[e, to_slot, half],
            device_id=(to, m), device_id_type=MESH,
        )

    def gather_up(e, half):
        return gather_copy(e, 0, 1, half, half, above)

    def gather_down(e, half):
        return gather_copy(e, 0, 2, half, 2 + half, below)

    def gather_on(e, half):
        return gather_copy(e, 1 + half, 3, half, 4 + half, (above, below)[half])

    def arrive(e, half):
        lo, hi = max(1, half * 16) * MSG, (half + 1) * 16 * MSG
        whole(e, came, e, lo, hi, a_send.at[e], a_recv.at[e, half]).wait_recv()
        unpack(came, e, half, rows.at[e, 0:ROWS])
        gather_up(e, half).start()
        gather_down(e, half).start()

    def pass_on(e):
        gather_up(e, 0).wait_recv()
        gather_on(e, 0).start()
        gather_down(e, 1).wait_recv()
        gather_on(e, 1).start()

    def gathered(e):
        gather_up(e, 1).wait_recv()
        gather_down(e, 0).wait_recv()
        for half in range(2):
            gather_on(e, half).wait_recv()

    def multiply(e, s):
        acc[...] = jnp.zeros_like(acc)

        @pl.loop(0, 8)
        def _(k):
            at = pl.ds(pl.multiple_of(k * 512, 512), 512)
            acc[...] += jnp.dot(rows[e, :, at], wide[s, at, :], preferred_element_type=F32)

        @pl.loop(0, 8)
        def _(i):
            at = pl.ds(pl.multiple_of(i * HALF, HALF), HALF)
            gate = acc[at, 0:Q]
            hidden[at, :] = (gate / (1.0 + jnp.exp(-gate)) * acc[at, Q : 2 * Q]).astype(BF16)

        @pl.loop(0, 8)
        def _(j):
            cols = pl.ds(pl.multiple_of(j * 512, 512), 512)
            part[e, s, :, cols] = jnp.dot(
                hidden[...], down[s, :, cols], preferred_element_type=F32
            ).astype(BF16)

    def at_part(e, s, slot, half):
        return part.at[e, s, slot * ROWS + half * HALF : slot * ROWS + (half + 1) * HALF]

    def copy_back(e, s, which):
        def to(source, target, n, recv_sem, device):
            return pltpu.make_async_remote_copy(
                source, target, p_send.at[e, s, n], recv_sem,
                device_id=(device, m), device_id_type=MESH,
            )

        def at_relay(k):
            return relay.at[e, s, k * HALF : (k + 1) * HALF]

        def at_home(k, half):
            return home.at[e, s, k, half * HALF : (half + 1) * HALF]

        if which < 2:
            half, device = which, (below, above)[which]
            return to(at_part(e, s, 3, half), at_relay(half), which, r_recv.at[e, s, half], device)
        k, half = ((0, 1), (1, 0), (0, 0), (1, 1))[which - 2]
        return to(
            at_part(e, s, 1 + k, half), at_home(k, half), which, h_recv.at[e, s, k, half],
            (below, above)[k],
        )

    def start_back(e, s):
        for which in range(4):
            copy_back(e, s, which).start()

    def relay_back(e, s):
        for k in range(2):
            copy_back(e, s, k).wait_recv()
            first = (1 + k) * ROWS + k * HALF

            @pl.loop(0, 8)
            def _(j):
                cols = pl.ds(pl.multiple_of(j * 512, 512), 512)
                part[e, s, first : first + HALF, cols] = (
                    part[e, s, first : first + HALF, cols].astype(F32)
                    + relay[e, s, k * HALF : (k + 1) * HALF, cols].astype(F32)
                ).astype(BF16)

            copy_back(e, s, 4 + k).start()

    def finish_back(e, s):
        for which in range(2, 6):
            copy_back(e, s, which).wait_recv()

        @pl.loop(0, 8)
        def _(j):
            cols = pl.ds(pl.multiple_of(j * 512, 512), 512)
            part[e, s, 0:ROWS, cols] = (
                part[e, s, 0:ROWS, cols].astype(F32)
                + home[e, s, 0, :, cols].astype(F32)
                + home[e, s, 1, :, cols].astype(F32)
            ).astype(BF16)

        i = 2 * e + s
        for half in range(2):
            pack(part.at[e, s], sent, i, half)
            exchange(i, back, i, 1, half, b_send.at[i], b_recv.at[i])
        back[i, 0:MSG, :] = sent[i, 0:MSG, :]

    loads = list(load_weights(0))
    loads[0].wait()
    loads[1].wait()
    move_wide(0, 0, 32)
    arrive(0, 0)
    arrive(0, 1)
    move_wide(0, 32, 96)
    pass_on(0)
    arrive(1, 0)
    arrive(1, 1)
    move_wide(0, 96, 128)
    loads[2].wait()
    move_down(0, 0, 96)
    gathered(0)
    multiply(0, 0)
    start_back(0, 0)
    multiply(0, 1)
    start_back(0, 1)
    for e in range(2):
        whole(e, came, e, MSG, PEERS * MSG, a_send.at[e], a_recv.at[e, 0]).wait_send()
    loads = list(load_weights(1))
    for copy in loads:
        copy.start()
    pass_on(1)
    loads[0].wait()
    loads[1].wait()
    move_wide(1, 0, 64)
    relay_back(0, 0)
    move_wide(1, 64, 128)
    loads[2].wait()
    relay_back(0, 1)
    move_down(1, 0, 96)
    gathered(1)
    multiply(1, 0)
    start_back(1, 0)
    multiply(1, 1)
    start_back(1, 1)
    finish_back(0, 0)
    finish_back(0, 1)
    relay_back(1, 0)
    relay_back(1, 1)
    finish_back(1, 0)
    finish_back(1, 1)

    for e in range(2):
        for half in range(2):
            for copy in (gather_up(e, half), gather_down(e, half), gather_on(e, half)):
                copy.wait_send()
        for s in range(2):
            for which in range(6):
                copy_back(e, s, which).wait_send()

    chosen = [
        jnp.where(
            key_col == slot_keys(*[slots_row[i : i + 1, :] for i in range(4)], e), 1.0, 0.0
        ).astype(BF16)
        for e in range(2)
    ]
    for s in range(2):
        for e in range(2):
            i = 2 * e + s
            whole(i, back, i, MSG, PEERS * MSG, b_send.at[i], b_recv.at[i]).wait()
            for half in range(2):
                unpack(back, i, half, part.at[e, s])

        @pl.loop(0, 4)
        def _(j):
            cols = pl.ds(pl.multiple_of(j * 1024, 1024), 1024)
            picked = jnp.dot(
                chosen[0], part[0, s, 0:ROWS, cols], preferred_element_type=F32
            ) + jnp.dot(chosen[1], part[1, s, 0:ROWS, cols], preferred_element_type=F32)
            part[0, s, ROWS : ROWS + 128, cols] = (probs[...] * picked).astype(BF16)

        target = (out_plus, out_minus)[s]
        pltpu.make_async_copy(part.at[0, s, ROWS : ROWS + 128], target, o_sem.at[s]).start()
    for s in range(2):
        target = (out_plus, out_minus)[s]
        pltpu.make_async_copy(part.at[0, s, ROWS : ROWS + 128], target, o_sem.at[s]).wait()


def shards(tokens, expert_ids, gate_probs, gate_weight, up_weight, down_weight, sign_offset):
    at = np.arange(768)
    swap = (at % 48 // 3 * 48 + at // 48 * 3 + at % 3).astype(np.int32).reshape(768, 1)
    slot = np.arange(ROWS)
    peer = slot // CAP
    slots = np.stack([peer // 8, peer // 2 % 4, peer % 2, slot % CAP], axis=1).astype(np.int32)
    vmem, hbm = pl.BlockSpec(memory_space=pltpu.VMEM), pl.BlockSpec(memory_space=pl.ANY)
    smem = pl.BlockSpec(memory_space=pltpu.SMEM)
    dma = pltpu.SemaphoreType.DMA
    return pl.pallas_call(
        kernel,
        out_shape=[jax.ShapeDtypeStruct((128, D), BF16)] * 2,
        in_specs=[vmem, vmem, vmem, smem, vmem, vmem, vmem, vmem, hbm, hbm, hbm],
        out_specs=[hbm, hbm],
        scratch_shapes=[
            pltpu.VMEM((2, 4 * ROWS, D), BF16),
            pltpu.VMEM((4, PEERS * MSG, 256), BF16),
            pltpu.VMEM((2, PEERS * MSG, 256), BF16),
            pltpu.VMEM((2, D, 2 * Q), BF16),
            pltpu.VMEM((2, Q, D), BF16),
            pltpu.VMEM((2, 2, 4 * ROWS, D), BF16),
            pltpu.VMEM((2, 2, ROWS, D), BF16),
            pltpu.VMEM((2, 2, 2, ROWS, D), BF16),
            pltpu.VMEM((4, PEERS * MSG, 256), BF16),
            pltpu.VMEM((4 * ROWS, 2 * Q), F32),
            pltpu.VMEM((4 * ROWS, Q), BF16),
            pltpu.VMEM((768, 768), BF16),
            dma((3,)),
            dma((2,)),
            dma((2, 2)),
            dma((2, 6)),
            dma((2, 4, 2)),
            dma((2, 2, 6)),
            dma((2, 2, 2)),
            dma((2, 2, 2, 2)),
            dma((4,)),
            dma((4,)),
            dma((2,)),
        ],
        compiler_params=pltpu.CompilerParams(
            collective_id=0, has_side_effects=True, vmem_limit_bytes=63_000_000
        ),
    )(
        expert_ids.reshape(1, 128),
        expert_ids,
        gate_probs,
        sign_offset,
        jnp.asarray(swap),
        jnp.asarray(slots),
        jnp.asarray(slots.T),
        tokens,
        gate_weight,
        up_weight,
        down_weight,
    )


def solution(mesh):
    in_specs = (
        P(("dp", "mp"), None),
        P(("dp", "mp"), None),
        P(("dp", "mp"), None),
        P("mp", None, "dp"),
        P("mp", None, "dp"),
        P("mp", "dp", None),
        P(),
    )
    out_specs = (P(("dp", "mp"), None), P(("dp", "mp"), None))
    return jax.shard_map(shards, mesh=mesh, in_specs=in_specs, out_specs=out_specs, check_vma=False)
```

profile of v0, /device:TPU:1, one launch (start us, length us, event | category | flops | bytes accessed | tf_op | source)
XLA Modules:
  0.0 201.5 jit_solution(17488187483042686664)
XLA Ops:
  1.3 1.4 copy.13.probs
  2.7 1.4 copy.12.ids_col
  4.1 192.8 %shard_map.113 = (bf16[128,4096]{1,0:T(8,128)(2,1)}, bf16[128,4096]{1,0:T(8,128)(2,1)}) custom-call(s32[1,128]{1,0:T(1,128)} %bitcast.1, s32[128,1]{1,0:T(8,128)} %copy.12.ids_col, f32[128,1]{1,0:T(8,128)} %copy.13.probs, s32[1]{0:T(128)S(6)} %copy.16.sign_offset, s32[768,1]{1,0:T(8,128)} %constant.6.clone.swap, s32[96,4]{1,0:T(8,128)} %constant.7.clone.slots_col, ...), custom_call_target="tpu_custom_call" | custom-call | tf_op jit(solution)/shard_map/pallas_call | solution.py:389
  196.9 2.3 %copy.17 = bf16[128,4096]{1,0:T(8,128)(2,1)} copy(bf16[128,4096]{1,0:T(8,128)(2,1)} %get-tuple-element.4) | data formatting | bytes 2097152
  199.2 2.3 %copy.18 = bf16[128,4096]{1,0:T(8,128)(2,1)} copy(bf16[128,4096]{1,0:T(8,128)(2,1)} %get-tuple-element.5) | data formatting | bytes 2097152
where the time goes:
time: 202 us; the launch traced here: 201 us
  Pallas kernels  193 us (96%)
  local copies, waits for them, and re-layouts  7.35 us (4%)
    pallas_call x1, Pallas kernels, shards(): pl.pallas_call(kernel, out_shape=[jax.ShapeDtypeStruct((128, D), BF16)] *...  193 us
    unnamed x4, local copies, waits for them, and re-layouts  7.35 us

commit v1 on v0

v1 whole, which is shorter than its diff:
```python
import jax
import jax.numpy as jnp
import numpy as np
from jax import lax
from jax.experimental import pallas as pl
from jax.experimental.pallas import tpu as pltpu
from jax.sharding import PartitionSpec as P

D = 4096
FF = 1536
Q = 384
CAP = 3
ROWS = 96
HALF = 48
WIDTH = 2048
MSG = 48
PEERS = 32
EPS = 0.005
MESH = pl.DeviceIdType.MESH
F32, BF16, I32 = jnp.float32, jnp.bfloat16, jnp.int32


def mixing(number):
    number = number ^ lax.shift_right_logical(number, jnp.full_like(number, 16))
    number = number * 73244475
    number = number ^ lax.shift_right_logical(number, jnp.full_like(number, 16))
    number = number * 73244475
    return number ^ lax.shift_right_logical(number, jnp.full_like(number, 16))


def moved_by(position, offset_mixed):
    hashed = mixing(position ^ offset_mixed)
    return jnp.where((hashed & 512) != 0, EPS, -EPS).astype(F32)


def kernel(
    ids_row, probs_row, sign_offset, swap, slots_col, slots_row, tokens, gate_w, up_w, down_w,
    out_plus, out_minus,
    ids_all, others, rows, sent_t, came_t, back_t, sent_s, came_s, back_s, wide, down, part_t, part_s,
    relay_s, home_s, relay_t, home_t, acc, hidden, perm,
    w_sem, i_send, i_recv, t_send, t_recv, xs_send, xs_recv, xt_send, xt_recv, z_send, z_recv,
    ps_send, rs_recv, hs_recv, pt_send, rt_recv, ht_recv, bs_send, bs_recv, bt_send, bt_recv, o_sem,
    free_sem,
):
    z, m = lax.axis_index("dp"), lax.axis_index("mp")
    x, y, core = m // 8, (m // 2) % 4, m % 2
    above, below, across = (z + 1) % 4, (z + 3) % 4, (z + 2) % 4
    hidden_base = z * Q

    def peer(p, sign):
        return (
            (x + sign * (p // 8) + 4) % 4 * 8
            + (y + sign * ((p // 2) % 4) + 4) % 4 * 2
            + (core + p) % 2
        )

    def remote(source, target, send_sem, recv_sem, device):
        return pltpu.make_async_remote_copy(
            source, target, send_sem, recv_sem, device_id=device, device_id_type=MESH
        )

    def load_weights(e):
        return [
            pltpu.make_async_copy(source.at[e], target, w_sem.at[i])
            for i, (source, target) in enumerate(
                (
                    (gate_w, wide.at[0, :, 0:Q]),
                    (up_w, wide.at[0, :, Q : 2 * Q]),
                    (down_w, down.at[0]),
                )
            )
        ]

    loads = load_weights(0)
    for copy in loads:
        copy.start()

    barrier = pltpu.get_barrier_semaphore()

    @pl.loop(1, PEERS)
    def _(p):
        pl.semaphore_signal(barrier, inc=1, device_id=(z, peer(p, -1)), device_id_type=MESH)

    for near in (above, below, across):
        pl.semaphore_signal(barrier, inc=1, device_id=(near, m), device_id_type=MESH)
    ids_all[0] = jnp.broadcast_to(ids_row[...], (8, 128))
    pl.semaphore_wait(barrier, PEERS + 2)

    def token_copy(up, half):
        at = slice(half * 64, half * 64 + 64)
        return remote(
            tokens.at[at, 0:WIDTH], others.at[0 if up else 1, at], t_send.at[0 if up else 1, half],
            t_recv.at[0 if up else 1, half], (above if up else below, m),
        )

    def token_on(half):
        at = slice(half * 64, half * 64 + 64)
        return remote(
            others.at[half, at], others.at[2, at], t_send.at[2, half], t_recv.at[2, half],
            ((above, below)[half], m),
        )

    def id_copy(slot):
        device = (above, below, across)[slot - 1]
        return remote(
            ids_all.at[0], ids_all.at[slot], i_send.at[slot - 1], i_recv.at[slot - 1], (device, m)
        )

    for slot in (1, 2, 3):
        id_copy(slot).start()
    for half in range(2):
        token_copy(True, half).start()
        token_copy(False, 1 - half).start()

    at_row = lax.broadcasted_iota(I32, (128, 128), 0)
    at_col = lax.broadcasted_iota(I32, (128, 128), 1)

    def as_column(row):
        return jnp.sum(jnp.where(at_row == at_col, row, jnp.zeros_like(row)), axis=1, keepdims=True)

    def keys(slot):
        row = ids_all[slot][0:1]
        column = as_column(row)
        alike = column == row
        key_col = column * 4 + jnp.sum(
            jnp.where(alike & (at_col < at_row), 1, 0), axis=1, keepdims=True
        )
        key_row = row * 4 + jnp.sum(
            jnp.where(alike & (at_row < at_col), 1, 0), axis=0, keepdims=True
        )
        return key_col, key_row

    def slot_keys(a, b, d, s, e):
        owner = ((x - a) & 3) * 8 + ((y - b) & 3) * 2 + ((core + d) & 1)
        return (owner * 2 + e) * 4 + s

    def one_hot(found):
        return jnp.where(found, 1.0, 0.0).astype(BF16)

    def to_slots(key_row, e):
        return one_hot(key_row == slot_keys(*[slots_col[:, i : i + 1] for i in range(4)], e))

    def to_tokens(key_col, e):
        return one_hot(key_col == slot_keys(*[slots_row[i : i + 1, :] for i in range(4)], e))

    perm[...] = one_hot(lax.broadcasted_iota(I32, (768, 768), 1) == swap[...])

    def swapped(value):
        return jnp.dot(perm[...], value, preferred_element_type=F32).astype(BF16)

    def piece(ref, slot, half, c):
        first = slot * ROWS + half * HALF
        return ref[first : first + HALF, c * 128 : (c + 1) * 128]

    def pack_s(source, target):
        laid = swapped(
            jnp.concatenate(
                [
                    jnp.concatenate([piece(source, 0, half, c) for half in range(2)], axis=1)
                    for c in range(16)
                ],
                axis=0,
            )
        )
        for half in range(2):
            target[half * 768 : (half + 1) * 768, :] = laid[:, half * 128 : (half + 1) * 128]

    def unpack_s(source, target, left):
        laid = swapped(jnp.concatenate([source[0:768, :], source[768:1536, :]], axis=1))
        for half in range(2):
            for c in range(16):
                target[
                    half * HALF : (half + 1) * HALF, left + c * 128 : left + (c + 1) * 128
                ] = laid[c * HALF : (c + 1) * HALF, half * 128 : (half + 1) * 128]

    def pack_t(source, target):
        for half in range(2):
            target[half * 768 : (half + 1) * 768, :] = swapped(
                jnp.concatenate(
                    [
                        jnp.concatenate([piece(source, slot, half, c) for slot in range(4)], axis=1)
                        for c in range(16)
                    ],
                    axis=0,
                )
            )

    def unpack_t(source, target, left):
        for half in range(2):
            laid = swapped(source[half * 768 : (half + 1) * 768, :])
            for slot in range(4):
                for c in range(16):
                    first = slot * ROWS + half * HALF
                    target[first : first + HALF, left + c * 128 : left + (c + 1) * 128] = laid[
                        c * HALF : (c + 1) * HALF, slot * 128 : (slot + 1) * 128
                    ]

    def exchange(source, target, send_sem, recv_sem, sign):
        @pl.loop(1, PEERS)
        def _(p):
            at = pl.ds(pl.multiple_of(p * MSG, MSG), MSG)
            remote(
                source.at[at], target.at[at], send_sem, recv_sem, (z, peer(p, sign))
            ).start()

        target[0:MSG, :] = source[0:MSG, :]

    def exchanged(source, target, send_sem, recv_sem):
        return remote(
            source.at[MSG : PEERS * MSG], target.at[MSG : PEERS * MSG], send_sem, recv_sem,
            (z, peer(1, 1)),
        )

    def out_s(e):
        return sent_s.at[e], came_s.at[e], xs_send.at[e], xs_recv.at[e]

    def out_t(e):
        return sent_t.at[e], came_t.at[e], xt_send.at[e], xt_recv.at[e]

    def home_of(e, s, sent, came, back, send_sem, recv_sem):
        i = 2 * e + s
        if e == 0:
            return sent.at[2 + s], back.at[s], send_sem.at[i], recv_sem.at[i]
        return sent.at[s], came.at[s], send_sem.at[i], recv_sem.at[i]

    def in_s(e, s):
        return home_of(e, s, sent_s, came_s, back_s, bs_send, bs_recv)

    def in_t(e, s):
        return home_of(e, s, sent_t, came_t, back_t, bt_send, bt_recv)

    key = [keys(0)]
    for e in range(2):
        chosen = to_slots(key[0][1], e)
        staged = part_s.at[0, e]
        for c in range(2):
            staged[0:ROWS, c * 1024 : (c + 1) * 1024] = jnp.dot(
                chosen,
                tokens[:, WIDTH + c * 1024 : WIDTH + (c + 1) * 1024],
                preferred_element_type=F32,
            ).astype(BF16)
        pack_s(staged, sent_s.at[e])
        exchange(*out_s(e), -1)

    offset_mixed = mixing(sign_offset[0] * 668265261 + 12345)

    def move_wide(e, lo, hi):
        expert = m * 2 + e
        inner = lax.broadcasted_iota(I32, (32, Q), 0) * (3 * FF) + lax.broadcasted_iota(
            I32, (32, Q), 1
        ) * 3

        @pl.loop(lo, hi)
        def _(i):
            at = pl.ds(pl.multiple_of(i * 32, 32), 32)
            first = ((expert * D + i * 32) * FF + hidden_base) * 3
            for tag in range(2):
                cols = slice(tag * Q, (tag + 1) * Q)
                weight = wide[0, at, cols].astype(F32)
                step = moved_by(inner + (first + tag), offset_mixed)
                wide[0, at, cols] = (weight + step).astype(BF16)
                wide[1, at, cols] = (weight - step).astype(BF16)

    def move_down(e, lo, hi):
        expert = m * 2 + e
        inner = lax.broadcasted_iota(I32, (32, 512), 0) * (3 * D) + lax.broadcasted_iota(
            I32, (32, 512), 1
        ) * 3

        @pl.loop(lo, hi)
        def _(i):
            row, col = i // 8 * 32, i % 8 * 512
            at, cols = pl.ds(pl.multiple_of(row, 32), 32), pl.ds(pl.multiple_of(col, 512), 512)
            first = ((expert * FF + hidden_base + row) * D + col) * 3 + 2
            weight = down[0, at, cols].astype(F32)
            step = moved_by(inner + first, offset_mixed)
            down[0, at, cols] = (weight + step).astype(BF16)
            down[1, at, cols] = (weight - step).astype(BF16)

    def tokens_on():
        token_copy(True, 0).wait_recv()
        token_on(0).start()
        token_copy(False, 1).wait_recv()
        token_on(1).start()

    def tokens_there():
        token_copy(True, 1).wait_recv()
        token_copy(False, 0).wait_recv()
        for half in range(2):
            token_on(half).wait_recv()
        for slot in (1, 2, 3):
            id_copy(slot).wait_recv()
            key.append(keys(slot))

    def dispatch_t(e):
        for slot in range(4):
            chosen = to_slots(key[slot][1], e)
            for c in range(2):
                cols = slice(c * 1024, (c + 1) * 1024)
                value = tokens[:, cols] if slot == 0 else others[slot - 1, :, cols]
                part_t[slot * ROWS : (slot + 1) * ROWS, cols] = jnp.dot(
                    chosen, value, preferred_element_type=F32
                ).astype(BF16)
        pack_t(part_t, sent_t.at[e])
        exchange(*out_t(e), -1)

    def arrive_t(e):
        exchanged(*out_t(e)).wait_recv()
        unpack_t(came_t.at[e], rows.at[e], 0)

    def arrive_s(e):
        exchanged(*out_s(e)).wait_recv()
        unpack_s(came_s.at[e], rows.at[e], WIDTH)

    def gather_copy(e, from_slot, to_slot, half, n, to):
        a, b = from_slot * ROWS + half * HALF, to_slot * ROWS + half * HALF
        return remote(
            rows.at[e, a : a + HALF, WIDTH:D], rows.at[e, b : b + HALF, WIDTH:D],
            z_send.at[e, n], z_recv.at[e, to_slot, half], (to, m),
        )

    def gather_up(e, half):
        return gather_copy(e, 0, 1, half, half, above)

    def gather_down(e, half):
        return gather_copy(e, 0, 2, half, 2 + half, below)

    def gather_on(e, half):
        return gather_copy(e, 1 + half, 3, half, 4 + half, (above, below)[half])

    def gather(e):
        for half in range(2):
            gather_up(e, half).start()
            gather_down(e, 1 - half).start()

    def pass_on(e):
        gather_up(e, 0).wait_recv()
        gather_on(e, 0).start()
        gather_down(e, 1).wait_recv()
        gather_on(e, 1).start()

    def gathered(e):
        gather_up(e, 1).wait_recv()
        gather_down(e, 0).wait_recv()
        for half in range(2):
            gather_on(e, half).wait_recv()

    def ring(block, relay, home, send_sem, relay_sem, home_sem):
        def copy(which):
            if which < 2:
                half = which
                return remote(
                    block(3, half), relay(half), send_sem.at[which], relay_sem.at[half],
                    ((below, above)[half], m),
                )
            k, half = ((0, 1), (1, 0), (0, 0), (1, 1))[which - 2]
            return remote(
                block(1 + k, half), home(k, half), send_sem.at[which], home_sem.at[k, half],
                ((below, above)[k], m),
            )

        def start():
            for which in range(4):
                copy(which).start()

        def pass_sum():
            for k in range(2):
                copy(k).wait_recv()
                mine, arrived = block(1 + k, k), relay(k)

                @pl.loop(0, 4)
                def _(j):
                    cols = pl.ds(pl.multiple_of(j * 512, 512), 512)
                    mine[:, cols] = (
                        mine[:, cols].astype(F32) + arrived[:, cols].astype(F32)
                    ).astype(BF16)

                copy(4 + k).start()

        def wait_home():
            for which in range(2, 6):
                copy(which).wait_recv()

        def wait_sent():
            for which in range(6):
                copy(which).wait_send()

        return start, pass_sum, wait_home, wait_sent

    def ring_s(e, s):
        def block(slot, half):
            return part_s.at[e, s, slot * ROWS + half * HALF : slot * ROWS + (half + 1) * HALF]

        return ring(
            block,
            lambda half: relay_s.at[e, s, half * HALF : (half + 1) * HALF],
            lambda k, half: home_s.at[e, s, k, half * HALF : (half + 1) * HALF],
            ps_send.at[e, s], rs_recv.at[e, s], hs_recv.at[e, s],
        )

    def block_t(s, slot, lo, hi):
        top, left = slot // 2 * 128, slot % 2 * WIDTH
        return down.at[s, top + lo : top + hi, left : left + WIDTH]

    def ring_t(s):
        return ring(
            lambda slot, half: block_t(s, slot, half * 64, half * 64 + 64),
            lambda half: relay_t.at[s, half * 64 : half * 64 + 64],
            lambda k, half: home_t.at[s, k, half * 64 : half * 64 + 64],
            pt_send.at[s], rt_recv.at[s], ht_recv.at[s],
        )

    def multiply(e, s):
        acc[...] = jnp.zeros_like(acc)

        @pl.loop(0, 8)
        def _(k):
            at = pl.ds(pl.multiple_of(k * 512, 512), 512)
            acc[...] += jnp.dot(rows[e, :, at], wide[s, at, :], preferred_element_type=F32)

        @pl.loop(0, 8)
        def _(i):
            at = pl.ds(pl.multiple_of(i * HALF, HALF), HALF)
            gate = acc[at, 0:Q]
            hidden[at, :] = (gate / (1.0 + jnp.exp(-gate)) * acc[at, Q : 2 * Q]).astype(BF16)

        def project(target, left):
            @pl.loop(0, 4)
            def _(j):
                cols = pl.ds(pl.multiple_of(j * 512, 512), 512)
                from_cols = pl.ds(pl.multiple_of(left + j * 512, 512), 512)
                target[:, cols] = jnp.dot(
                    hidden[...], down[s, :, from_cols], preferred_element_type=F32
                ).astype(BF16)

        project(part_s.at[e, s], WIDTH)
        ring_s(e, s)[0]()
        project(part_t, 0)
        source, target, send_sem, recv_sem = in_t(e, s)
        pack_t(part_t, source)
        exchange(source, target, send_sem, recv_sem, 1)

    def finish_s(e, s):
        ring_s(e, s)[2]()

        @pl.loop(0, 4)
        def _(j):
            cols = pl.ds(pl.multiple_of(j * 512, 512), 512)
            part_s[e, s, 0:ROWS, cols] = (
                part_s[e, s, 0:ROWS, cols].astype(F32)
                + home_s[e, s, 0, :, cols].astype(F32)
                + home_s[e, s, 1, :, cols].astype(F32)
            ).astype(BF16)

        source, target, send_sem, recv_sem = in_s(e, s)
        pack_s(part_s.at[e, s], source)
        exchange(source, target, send_sem, recv_sem, 1)

    def collect_t(s):
        for e in range(2):
            source, target, send_sem, recv_sem = in_t(e, s)
            exchanged(source, target, send_sem, recv_sem).wait_recv()
            unpack_t(target, rows.at[1], e * WIDTH)
        for slot in (3, 1, 2, 0):
            first, second = to_tokens(key[slot][0], 0), to_tokens(key[slot][0], 1)
            at = slice(slot * ROWS, (slot + 1) * ROWS)
            target = block_t(s, slot, 0, 128)

            @pl.loop(0, 2)
            def _(j):
                cols = pl.ds(pl.multiple_of(j * 1024, 1024), 1024)
                cols_1 = pl.ds(pl.multiple_of(WIDTH + j * 1024, 1024), 1024)
                target[:, cols] = (
                    jnp.dot(first, rows[1, at, cols], preferred_element_type=F32)
                    + jnp.dot(second, rows[1, at, cols_1], preferred_element_type=F32)
                ).astype(BF16)

        ring_t(s)[0]()

    def result_copy(s, n):
        source = (down.at[s, 0:128, 0:WIDTH], down.at[s, 256:384, WIDTH:D])[n]
        target = (out_plus, out_minus)[s].at[:, n * WIDTH : (n + 1) * WIDTH]
        return pltpu.make_async_copy(source, target, o_sem.at[s, n])

    def result_s(s):
        for e in range(2):
            source, target, send_sem, recv_sem = in_s(e, s)
            exchanged(source, target, send_sem, recv_sem).wait_recv()
            unpack_s(target, rows.at[0], e * WIDTH)
        first, second = to_tokens(key[0][0], 0), to_tokens(key[0][0], 1)

        @pl.loop(0, 2)
        def _(j):
            cols = pl.ds(pl.multiple_of(j * 1024, 1024), 1024)
            cols_1 = pl.ds(pl.multiple_of(WIDTH + j * 1024, 1024), 1024)
            picked = jnp.dot(
                first, rows[0, 0:ROWS, cols], preferred_element_type=F32
            ) + jnp.dot(second, rows[0, 0:ROWS, cols_1], preferred_element_type=F32)
            down[s, 256:384, cols_1] = (probs * picked).astype(BF16)

        result_copy(s, 1).start()

    def result_t(s):
        ring_t(s)[2]()

        @pl.loop(0, 4)
        def _(j):
            cols = pl.ds(pl.multiple_of(j * 512, 512), 512)
            summed = (
                down[s, 0:128, cols].astype(F32)
                + home_t[s, 0, :, cols].astype(F32)
                + home_t[s, 1, :, cols].astype(F32)
            ).astype(BF16)
            down[s, 0:128, cols] = (probs * summed.astype(F32)).astype(BF16)

        result_copy(s, 0).start()

    probs = as_column(probs_row[...])
    loads[0].wait()
    loads[1].wait()
    move_wide(0, 0, 24)
    tokens_on()
    arrive_s(0)
    gather(0)
    move_wide(0, 24, 48)
    tokens_there()
    dispatch_t(0)
    dispatch_t(1)
    arrive_s(1)
    move_wide(0, 48, 72)
    pass_on(0)
    gather(1)
    move_wide(0, 72, 128)
    loads[2].wait()
    move_down(0, 0, 96)
    pass_on(1)
    gathered(0)
    arrive_t(0)
    multiply(0, 0)
    multiply(0, 1)
    loads = load_weights(1)
    for copy in loads:
        copy.start()
    arrive_t(1)

    @pl.loop(1, PEERS)
    def _(p):
        pl.semaphore_signal(free_sem, inc=1, device_id=(z, peer(p, -1)), device_id_type=MESH)

    loads[0].wait()
    loads[1].wait()
    move_wide(1, 0, 32)
    ring_s(0, 0)[1]()
    move_wide(1, 32, 96)
    ring_s(0, 1)[1]()
    move_wide(1, 96, 128)
    loads[2].wait()
    move_down(1, 0, 48)
    finish_s(0, 0)
    move_down(1, 48, 96)
    gathered(1)
    for e in range(2):
        exchanged(*out_t(e)).wait_send()
        exchanged(*out_s(e)).wait_send()
        for half in range(2):
            for copy in (gather_up(e, half), gather_down(e, half), gather_on(e, half)):
                copy.wait_send()
    pl.semaphore_wait(free_sem, PEERS - 1)
    multiply(1, 0)
    multiply(1, 1)
    finish_s(0, 1)
    ring_s(1, 0)[1]()
    ring_s(1, 1)[1]()
    collect_t(0)
    finish_s(1, 0)
    ring_t(0)[1]()
    finish_s(1, 1)
    collect_t(1)
    result_s(0)
    ring_t(1)[1]()
    result_t(0)
    result_s(1)
    result_t(1)

    for slot in (1, 2, 3):
        id_copy(slot).wait_send()
    for half in range(2):
        token_copy(True, half).wait_send()
        token_copy(False, half).wait_send()
        token_on(half).wait_send()
    for e in range(2):
        for s in range(2):
            ring_s(e, s)[3]()
            exchanged(*in_s(e, s)).wait_send()
            exchanged(*in_t(e, s)).wait_send()
    for s in range(2):
        ring_t(s)[3]()
        for n in range(2):
            result_copy(s, n).wait()


def shards(tokens, expert_ids, gate_probs, gate_weight, up_weight, down_weight, sign_offset):
    at = np.arange(768)
    swap = (at % 48 // 3 * 48 + at // 48 * 3 + at % 3).astype(np.int32).reshape(768, 1)
    slot = np.arange(ROWS)
    peer = slot // CAP
    slots = np.stack([peer // 8, peer // 2 % 4, peer % 2, slot % CAP], axis=1).astype(np.int32)
    vmem, hbm = pl.BlockSpec(memory_space=pltpu.VMEM), pl.BlockSpec(memory_space=pl.ANY)
    smem = pl.BlockSpec(memory_space=pltpu.SMEM)
    dma = pltpu.SemaphoreType.DMA
    return pl.pallas_call(
        kernel,
        out_shape=[jax.ShapeDtypeStruct((128, D), BF16)] * 2,
        in_specs=[vmem, vmem, smem, vmem, vmem, vmem, vmem, hbm, hbm, hbm],
        out_specs=[hbm, hbm],
        scratch_shapes=[
            pltpu.VMEM((4, 8, 128), I32),
            pltpu.VMEM((3, 128, WIDTH), BF16),
            pltpu.VMEM((2, 4 * ROWS, D), BF16),
            pltpu.VMEM((4, PEERS * MSG, 512), BF16),
            pltpu.VMEM((2, PEERS * MSG, 512), BF16),
            pltpu.VMEM((2, PEERS * MSG, 512), BF16),
            pltpu.VMEM((4, PEERS * MSG, 128), BF16),
            pltpu.VMEM((2, PEERS * MSG, 128), BF16),
            pltpu.VMEM((2, PEERS * MSG, 128), BF16),
            pltpu.VMEM((2, D, 2 * Q), BF16),
            pltpu.VMEM((2, Q, D), BF16),
            pltpu.VMEM((4 * ROWS, WIDTH), BF16),
            pltpu.VMEM((2, 2, 4 * ROWS, WIDTH), BF16),
            pltpu.VMEM((2, 2, ROWS, WIDTH), BF16),
            pltpu.VMEM((2, 2, 2, ROWS, WIDTH), BF16),
            pltpu.VMEM((2, 128, WIDTH), BF16),
            pltpu.VMEM((2, 2, 128, WIDTH), BF16),
            pltpu.VMEM((4 * ROWS, 2 * Q), F32),
            pltpu.VMEM((4 * ROWS, Q), BF16),
            pltpu.VMEM((768, 768), BF16),
            dma((3,)),
            dma((3,)),
            dma((3,)),
            dma((3, 2)),
            dma((3, 2)),
            dma((2,)),
            dma((2,)),
            dma((2,)),
            dma((2,)),
            dma((2, 6)),
            dma((2, 4, 2)),
            dma((2, 2, 6)),
            dma((2, 2, 2)),
            dma((2, 2, 2, 2)),
            dma((2, 6)),
            dma((2, 2)),
            dma((2, 2, 2)),
            dma((4,)),
            dma((4,)),
            dma((4,)),
            dma((4,)),
            dma((2, 2)),
            pltpu.SemaphoreType.REGULAR,
        ],
        compiler_params=pltpu.CompilerParams(
            collective_id=0, has_side_effects=True, vmem_limit_bytes=65_500_000
        ),
    )(
        expert_ids.reshape(1, 128),
        gate_probs.reshape(1, 128),
        sign_offset,
        jnp.asarray(swap),
        jnp.asarray(slots),
        jnp.asarray(slots.T),
        tokens,
        gate_weight,
        up_weight,
        down_weight,
    )


def solution(mesh):
    in_specs = (
        P(("dp", "mp"), None),
        P(("dp", "mp"), None),
        P(("dp", "mp"), None),
        P("mp", None, "dp"),
        P("mp", None, "dp"),
        P("mp", "dp", None),
        P(),
    )
    out_specs = (P(("dp", "mp"), None), P(("dp", "mp"), None))
    return jax.shard_map(shards, mesh=mesh, in_specs=in_specs, out_specs=out_specs, check_vma=False)
```

time: 202 us -> 194 us (0.960)
  Pallas kernels: 193 us -> 188 us
  local copies, waits for them, and re-layouts: 7.35 us -> 4.57 us
    pallas_call x1, Pallas kernels: 193 us -> 188 us  [shards(): pl.pallas_call(kernel, out_shape=[jax.ShapeDtypeStruct((128, D), BF16)] *...]
    unnamed x4 -> x2, local copies, waits for them, and re-layouts: 7.35 us -> 4.57 us
where the time goes in v1:
time: 194 us
  Pallas kernels  188 us (97%)
  local copies, waits for them, and re-layouts  4.57 us (2%)
    pallas_call x1, Pallas kernels, shards(): pl.pallas_call(kernel, out_shape=[jax.ShapeDtypeStruct((128, D), BF16)] *...  188 us
    unnamed x2, local copies, waits for them, and re-layouts  4.57 us

profile of v1, /device:TPU:1, one launch (start us, length us, event | category | flops | bytes accessed | tf_op | source)
XLA Modules:
  0.0 193.9 jit_solution(5642553130823403501)
XLA Ops:
  1.3 188.1 %shard_map.113 = (bf16[128,4096]{1,0:T(8,128)(2,1)}, bf16[128,4096]{1,0:T(8,128)(2,1)}) custom-call(s32[1,128]{1,0:T(1,128)} %bitcast.2, f32[1,128]{1,0:T(1,128)} %bitcast.3, s32[1]{0:T(128)S(6)} %copy.14.sign_offset, s32[768,1]{1,0:T(8,128)} %constant.6.clone.swap, s32[96,4]{1,0:T(8,128)} %constant.7.clone.slots_col, s32[4,96]{1,0:T(4,128)} %constant.8.clone.slots_row, ...), custom_call_target="tpu_custom_call" | custom-call | tf_op jit(solution)/shard_map/pallas_call | solution.py:611
  189.4 2.3 %copy.15 = bf16[128,4096]{1,0:T(8,128)(2,1)} copy(bf16[128,4096]{1,0:T(8,128)(2,1)} %get-tuple-element.4) | data formatting | bytes 2097152
  191.7 2.3 %copy.16 = bf16[128,4096]{1,0:T(8,128)(2,1)} copy(bf16[128,4096]{1,0:T(8,128)(2,1)} %get-tuple-element.5) | data formatting | bytes 2097152

commit v2 on v1

--- a/solution.py
+++ b/solution.py
@@ -33,8 +33,15 @@
     return jnp.where((hashed & 512) != 0, EPS, -EPS).astype(F32)
 
 
+def weigh(probs_row, plus, minus, out_plus, out_minus):
+    same = lax.broadcasted_iota(I32, (128, 128), 0) == lax.broadcasted_iota(I32, (128, 128), 1)
+    probs = jnp.sum(jnp.where(same, probs_row[...], 0.0), axis=1, keepdims=True)
+    out_plus[...] = (probs * plus[...].astype(F32)).astype(BF16)
+    out_minus[...] = (probs * minus[...].astype(F32)).astype(BF16)
+
+
 def kernel(
-    ids_row, probs_row, sign_offset, swap, slots_col, slots_row, tokens, gate_w, up_w, down_w,
+    ids_row, sign_offset, swap, slots_col, slots_row, tokens, gate_w, up_w, down_w,
     out_plus, out_minus,
     ids_all, others, rows, sent_t, came_t, back_t, sent_s, came_s, back_s, wide, down, part_t, part_s,
     relay_s, home_s, relay_t, home_t, acc, hidden, perm,
@@ -43,15 +50,16 @@
     free_sem,
 ):
     z, m = lax.axis_index("dp"), lax.axis_index("mp")
-    x, y, core = m // 8, (m // 2) % 4, m % 2
+    x, y, core = lax.div(m, 8), lax.rem(lax.div(m, 2), 4), lax.rem(m, 2)
     above, below, across = (z + 1) % 4, (z + 3) % 4, (z + 2) % 4
     hidden_base = z * Q
 
     def peer(p, sign):
+        a, b = lax.div(p, 8), lax.rem(lax.div(p, 2), 4)
         return (
-            (x + sign * (p // 8) + 4) % 4 * 8
-            + (y + sign * ((p // 2) % 4) + 4) % 4 * 2
-            + (core + p) % 2
+            lax.rem(x + sign * a + 4, 4) * 8
+            + lax.rem(y + sign * b + 4, 4) * 2
+            + lax.rem(core + p, 2)
         )
 
     def remote(source, target, send_sem, recv_sem, device):
@@ -148,15 +156,20 @@
     def swapped(value):
         return jnp.dot(perm[...], value, preferred_element_type=F32).astype(BF16)
 
-    def piece(ref, slot, half, c):
-        first = slot * ROWS + half * HALF
-        return ref[first : first + HALF, c * 128 : (c + 1) * 128]
-
-    def pack_s(source, target):
+    def pack(source, first, target):
         laid = swapped(
             jnp.concatenate(
                 [
-                    jnp.concatenate([piece(source, 0, half, c) for half in range(2)], axis=1)
+                    jnp.concatenate(
+                        [
+                            source[
+                                first + half * HALF : first + (half + 1) * HALF,
+                                c * 128 : (c + 1) * 128,
+                            ]
+                            for half in range(2)
+                        ],
+                        axis=1,
+                    )
                     for c in range(16)
                 ],
                 axis=0,
@@ -165,35 +178,14 @@
         for half in range(2):
             target[half * 768 : (half + 1) * 768, :] = laid[:, half * 128 : (half + 1) * 128]
 
-    def unpack_s(source, target, left):
+    def unpack(source, target, first, left):
         laid = swapped(jnp.concatenate([source[0:768, :], source[768:1536, :]], axis=1))
         for half in range(2):
             for c in range(16):
                 target[
-                    half * HALF : (half + 1) * HALF, left + c * 128 : left + (c + 1) * 128
+                    first + half * HALF : first + (half + 1) * HALF,
+                    left + c * 128 : left + (c + 1) * 128,
                 ] = laid[c * HALF : (c + 1) * HALF, half * 128 : (half + 1) * 128]
-
-    def pack_t(source, target):
-        for half in range(2):
-            target[half * 768 : (half + 1) * 768, :] = swapped(
-                jnp.concatenate(
-                    [
-                        jnp.concatenate([piece(source, slot, half, c) for slot in range(4)], axis=1)
-                        for c in range(16)
-                    ],
-                    axis=0,
-                )
-            )
-
-    def unpack_t(source, target, left):
-        for half in range(2):
-            laid = swapped(source[half * 768 : (half + 1) * 768, :])
-            for slot in range(4):
-                for c in range(16):
-                    first = slot * ROWS + half * HALF
-                    target[first : first + HALF, left + c * 128 : left + (c + 1) * 128] = laid[
-                        c * HALF : (c + 1) * HALF, slot * 128 : (slot + 1) * 128
-                    ]
 
     def exchange(source, target, send_sem, recv_sem, sign):
         @pl.loop(1, PEERS)
@@ -208,39 +200,47 @@
     def exchanged(source, target, send_sem, recv_sem):
         return remote(
             source.at[MSG : PEERS * MSG], target.at[MSG : PEERS * MSG], send_sem, recv_sem,
-            (z, peer(1, 1)),
+            (z, peer(jnp.int32(1), 1)),
         )
 
     def out_s(e):
         return sent_s.at[e], came_s.at[e], xs_send.at[e], xs_recv.at[e]
 
-    def out_t(e):
-        return sent_t.at[e], came_t.at[e], xt_send.at[e], xt_recv.at[e]
-
-    def home_of(e, s, sent, came, back, send_sem, recv_sem):
+    def out_t(e, slot):
+        return sent_t.at[e, slot], came_t.at[e, slot], xt_send.at[e, slot], xt_recv.at[e, slot]
+
+    def in_s(e, s):
         i = 2 * e + s
         if e == 0:
-            return sent.at[2 + s], back.at[s], send_sem.at[i], recv_sem.at[i]
-        return sent.at[s], came.at[s], send_sem.at[i], recv_sem.at[i]
-
-    def in_s(e, s):
-        return home_of(e, s, sent_s, came_s, back_s, bs_send, bs_recv)
-
-    def in_t(e, s):
-        return home_of(e, s, sent_t, came_t, back_t, bt_send, bt_recv)
-
-    key = [keys(0)]
-    for e in range(2):
-        chosen = to_slots(key[0][1], e)
+            return sent_s.at[2 + s], back_s.at[s], bs_send.at[i], bs_recv.at[i]
+        return sent_s.at[s], came_s.at[s], bs_send.at[i], bs_recv.at[i]
+
+    def in_t(e, s, slot):
+        i = 2 * e + s
+        if e == 0:
+            return sent_t.at[2 + s, slot], back_t.at[s, slot], bt_send.at[i, slot], bt_recv.at[i, slot]
+        return sent_t.at[s, slot], came_t.at[s, slot], bt_send.at[i, slot], bt_recv.at[i, slot]
+
+    key = {0: keys(0)}
+
+    def select(e, slot, value, target, first):
+        chosen = to_slots(key[slot][1], e)
+        for c in range(2):
+            target[first : first + ROWS, c * 1024 : (c + 1) * 1024] = jnp.dot(
+                chosen, value(slice(c * 1024, (c + 1) * 1024)), preferred_element_type=F32
+            ).astype(BF16)
+
+    def dispatch_s(e):
         staged = part_s.at[0, e]
-        for c in range(2):
-            staged[0:ROWS, c * 1024 : (c + 1) * 1024] = jnp.dot(
-                chosen,
-                tokens[:, WIDTH + c * 1024 : WIDTH + (c + 1) * 1024],
-                preferred_element_type=F32,
-            ).astype(BF16)
-        pack_s(staged, sent_s.at[e])
+        select(e, 0, lambda cols: tokens[:, WIDTH + cols.start : WIDTH + cols.stop], staged, 0)
+        pack(staged, 0, sent_s.at[e])
         exchange(*out_s(e), -1)
+
+    def dispatch_t(e, slot):
+        value = (lambda cols: tokens[:, cols]) if slot == 0 else (lambda cols: others[slot - 1, :, cols])
+        select(e, slot, value, part_t, slot * ROWS)
+        pack(part_t, slot * ROWS, sent_t.at[e, slot])
+        exchange(*out_t(e, slot), -1)
 
     offset_mixed = mixing(sign_offset[0] * 668265261 + 12345)
 
@@ -283,34 +283,22 @@
         token_copy(False, 1).wait_recv()
         token_on(1).start()
 
-    def tokens_there():
-        token_copy(True, 1).wait_recv()
-        token_copy(False, 0).wait_recv()
-        for half in range(2):
-            token_on(half).wait_recv()
-        for slot in (1, 2, 3):
-            id_copy(slot).wait_recv()
-            key.append(keys(slot))
-
-    def dispatch_t(e):
-        for slot in range(4):
-            chosen = to_slots(key[slot][1], e)
-            for c in range(2):
-                cols = slice(c * 1024, (c + 1) * 1024)
-                value = tokens[:, cols] if slot == 0 else others[slot - 1, :, cols]
-                part_t[slot * ROWS : (slot + 1) * ROWS, cols] = jnp.dot(
-                    chosen, value, preferred_element_type=F32
-                ).astype(BF16)
-        pack_t(part_t, sent_t.at[e])
-        exchange(*out_t(e), -1)
-
-    def arrive_t(e):
-        exchanged(*out_t(e)).wait_recv()
-        unpack_t(came_t.at[e], rows.at[e], 0)
+    def tokens_there(slot):
+        if slot == 3:
+            for half in range(2):
+                token_on(half).wait_recv()
+        else:
+            token_copy(slot == 1, 2 - slot).wait_recv()
+        id_copy(slot).wait_recv()
+        key[slot] = keys(slot)
+
+    def arrive_t(e, slot):
+        exchanged(*out_t(e, slot)).wait_recv()
+        unpack(came_t.at[e, slot], rows.at[e], slot * ROWS, 0)
 
     def arrive_s(e):
         exchanged(*out_s(e)).wait_recv()
-        unpack_s(came_s.at[e], rows.at[e], WIDTH)
+        unpack(came_s.at[e], rows.at[e], 0, WIDTH)
 
     def gather_copy(e, from_slot, to_slot, half, n, to):
         a, b = from_slot * ROWS + half * HALF, to_slot * ROWS + half * HALF
@@ -359,9 +347,9 @@
                 ((below, above)[k], m),
             )
 
-        def start():
-            for which in range(4):
-                copy(which).start()
+        def start(*which):
+            for n in which:
+                copy(n).start()
 
         def pass_sum():
             for k in range(2):
@@ -434,11 +422,11 @@
                 ).astype(BF16)
 
         project(part_s.at[e, s], WIDTH)
-        ring_s(e, s)[0]()
+        ring_s(e, s)[0](0, 1, 2, 3)
         project(part_t, 0)
-        source, target, send_sem, recv_sem = in_t(e, s)
-        pack_t(part_t, source)
-        exchange(source, target, send_sem, recv_sem, 1)
+        for slot in (3, 1, 2, 0):
+            pack(part_t, slot * ROWS, in_t(e, s, slot)[0])
+            exchange(*in_t(e, s, slot), 1)
 
     def finish_s(e, s):
         ring_s(e, s)[2]()
@@ -452,30 +440,24 @@
                 + home_s[e, s, 1, :, cols].astype(F32)
             ).astype(BF16)
 
-        source, target, send_sem, recv_sem = in_s(e, s)
-        pack_s(part_s.at[e, s], source)
-        exchange(source, target, send_sem, recv_sem, 1)
+        pack(part_s.at[e, s], 0, in_s(e, s)[0])
+        exchange(*in_s(e, s), 1)
 
     def collect_t(s):
-        for e in range(2):
-            source, target, send_sem, recv_sem = in_t(e, s)
-            exchanged(source, target, send_sem, recv_sem).wait_recv()
-            unpack_t(target, rows.at[1], e * WIDTH)
         for slot in (3, 1, 2, 0):
+            for e in range(2):
+                exchanged(*in_t(e, s, slot)).wait_recv()
+                unpack(in_t(e, s, slot)[1], rows.at[1], slot * ROWS, e * WIDTH)
             first, second = to_tokens(key[slot][0], 0), to_tokens(key[slot][0], 1)
             at = slice(slot * ROWS, (slot + 1) * ROWS)
-            target = block_t(s, slot, 0, 128)
-
-            @pl.loop(0, 2)
-            def _(j):
-                cols = pl.ds(pl.multiple_of(j * 1024, 1024), 1024)
-                cols_1 = pl.ds(pl.multiple_of(WIDTH + j * 1024, 1024), 1024)
-                target[:, cols] = (
+            for j in range(2):
+                cols = slice(j * 1024, (j + 1) * 1024)
+                cols_1 = slice(WIDTH + j * 1024, WIDTH + (j + 1) * 1024)
+                block_t(s, slot, 0, 128)[:, cols] = (
                     jnp.dot(first, rows[1, at, cols], preferred_element_type=F32)
                     + jnp.dot(second, rows[1, at, cols_1], preferred_element_type=F32)
                 ).astype(BF16)
-
-        ring_t(s)[0]()
+            ring_t(s)[0](*{3: (0, 1), 1: (2,), 2: (3,), 0: ()}[slot])
 
     def result_copy(s, n):
         source = (down.at[s, 0:128, 0:WIDTH], down.at[s, 256:384, WIDTH:D])[n]
@@ -484,9 +466,8 @@
 
     def result_s(s):
         for e in range(2):
-            source, target, send_sem, recv_sem = in_s(e, s)
-            exchanged(source, target, send_sem, recv_sem).wait_recv()
-            unpack_s(target, rows.at[0], e * WIDTH)
+            exchanged(*in_s(e, s)).wait_recv()
+            unpack(in_s(e, s)[1], rows.at[0], 0, e * WIDTH)
         first, second = to_tokens(key[0][0], 0), to_tokens(key[0][0], 1)
 
         @pl.loop(0, 2)
@@ -496,7 +477,7 @@
             picked = jnp.dot(
                 first, rows[0, 0:ROWS, cols], preferred_element_type=F32
             ) + jnp.dot(second, rows[0, 0:ROWS, cols_1], preferred_element_type=F32)
-            down[s, 256:384, cols_1] = (probs * picked).astype(BF16)
+            down[s, 256:384, cols_1] = picked.astype(BF16)
 
         result_copy(s, 1).start()
 
@@ -506,42 +487,52 @@
         @pl.loop(0, 4)
         def _(j):
             cols = pl.ds(pl.multiple_of(j * 512, 512), 512)
-            summed = (
+            down[s, 0:128, cols] = (
                 down[s, 0:128, cols].astype(F32)
                 + home_t[s, 0, :, cols].astype(F32)
                 + home_t[s, 1, :, cols].astype(F32)
             ).astype(BF16)
-            down[s, 0:128, cols] = (probs * summed.astype(F32)).astype(BF16)
 
         result_copy(s, 0).start()
 
-    probs = as_column(probs_row[...])
+    dispatch_t(0, 0)
+    dispatch_s(0)
+    dispatch_t(1, 0)
     loads[0].wait()
     loads[1].wait()
     move_wide(0, 0, 24)
     tokens_on()
+    move_wide(0, 24, 56)
+    for slot in (1, 2):
+        tokens_there(slot)
+        dispatch_t(0, slot)
     arrive_s(0)
     gather(0)
-    move_wide(0, 24, 48)
-    tokens_there()
-    dispatch_t(0)
-    dispatch_t(1)
+    move_wide(0, 56, 88)
+    tokens_there(3)
+    dispatch_t(0, 3)
+    dispatch_s(1)
+    for slot in (1, 2, 3):
+        dispatch_t(1, slot)
+    move_wide(0, 88, 128)
+    pass_on(0)
+    loads[2].wait()
+    move_down(0, 0, 48)
+    arrive_t(0, 0)
     arrive_s(1)
-    move_wide(0, 48, 72)
-    pass_on(0)
     gather(1)
-    move_wide(0, 72, 128)
-    loads[2].wait()
-    move_down(0, 0, 96)
+    move_down(0, 48, 96)
+    for slot in (1, 2, 3):
+        arrive_t(0, slot)
+    gathered(0)
+    multiply(0, 0)
     pass_on(1)
-    gathered(0)
-    arrive_t(0)
-    multiply(0, 0)
     multiply(0, 1)
     loads = load_weights(1)
     for copy in loads:
         copy.start()
-    arrive_t(1)
+    for slot in range(4):
+        arrive_t(1, slot)
 
     @pl.loop(1, PEERS)
     def _(p):
@@ -560,7 +551,8 @@
     move_down(1, 48, 96)
     gathered(1)
     for e in range(2):
-        exchanged(*out_t(e)).wait_send()
+        for slot in range(4):
+            exchanged(*out_t(e, slot)).wait_send()
         exchanged(*out_s(e)).wait_send()
         for half in range(2):
             for copy in (gather_up(e, half), gather_down(e, half), gather_on(e, half)):
@@ -592,7 +584,8 @@
         for s in range(2):
             ring_s(e, s)[3]()
             exchanged(*in_s(e, s)).wait_send()
-            exchanged(*in_t(e, s)).wait_send()
+            for slot in range(4):
+                exchanged(*in_t(e, s, slot)).wait_send()
     for s in range(2):
         ring_t(s)[3]()
         for n in range(2):
@@ -608,18 +601,18 @@
     vmem, hbm = pl.BlockSpec(memory_space=pltpu.VMEM), pl.BlockSpec(memory_space=pl.ANY)
     smem = pl.BlockSpec(memory_space=pltpu.SMEM)
     dma = pltpu.SemaphoreType.DMA
-    return pl.pallas_call(
+    plus, minus = pl.pallas_call(
         kernel,
         out_shape=[jax.ShapeDtypeStruct((128, D), BF16)] * 2,
-        in_specs=[vmem, vmem, smem, vmem, vmem, vmem, vmem, hbm, hbm, hbm],
+        in_specs=[vmem, smem, vmem, vmem, vmem, vmem, hbm, hbm, hbm],
         out_specs=[hbm, hbm],
         scratch_shapes=[
             pltpu.VMEM((4, 8, 128), I32),
             pltpu.VMEM((3, 128, WIDTH), BF16),
             pltpu.VMEM((2, 4 * ROWS, D), BF16),
-            pltpu.VMEM((4, PEERS * MSG, 512), BF16),
-            pltpu.VMEM((2, PEERS * MSG, 512), BF16),
-            pltpu.VMEM((2, PEERS * MSG, 512), BF16),
+            pltpu.VMEM((4, 4, PEERS * MSG, 128), BF16),
+            pltpu.VMEM((2, 4, PEERS * MSG, 128), BF16),
+            pltpu.VMEM((2, 4, PEERS * MSG, 128), BF16),
             pltpu.VMEM((4, PEERS * MSG, 128), BF16),
             pltpu.VMEM((2, PEERS * MSG, 128), BF16),
             pltpu.VMEM((2, PEERS * MSG, 128), BF16),
@@ -641,8 +634,8 @@
             dma((3, 2)),
             dma((2,)),
             dma((2,)),
-            dma((2,)),
-            dma((2,)),
+            dma((2, 4)),
+            dma((2, 4)),
             dma((2, 6)),
             dma((2, 4, 2)),
             dma((2, 2, 6)),
@@ -653,8 +646,8 @@
             dma((2, 2, 2)),
             dma((4,)),
             dma((4,)),
-            dma((4,)),
-            dma((4,)),
+            dma((4, 4)),
+            dma((4, 4)),
             dma((2, 2)),
             pltpu.SemaphoreType.REGULAR,
         ],
@@ -663,7 +656,6 @@
         ),
     )(
         expert_ids.reshape(1, 128),
-        gate_probs.reshape(1, 128),
         sign_offset,
         jnp.asarray(swap),
         jnp.asarray(slots),
@@ -673,6 +665,14 @@
         up_weight,
         down_weight,
     )
+    block = pl.BlockSpec((128, 1024), lambda i: (0, i))
+    return pl.pallas_call(
+        weigh,
+        out_shape=[jax.ShapeDtypeStruct((128, D), BF16)] * 2,
+        grid=(4,),
+        in_specs=[pl.BlockSpec((1, 128), lambda i: (0, 0)), block, block],
+        out_specs=[block, block],
+    )(gate_probs.reshape(1, 128), plus, minus)
 
 
 def solution(mesh):

time: 194 us -> 175 us (0.902)
  Pallas kernels: 188 us -> 174 us
  local copies, waits for them, and re-layouts: 4.57 us -> 0 us
    pallas_call x1, Pallas kernels: 188 us -> 170 us  [shards(): pl.pallas_call(kernel, out_shape=[jax.ShapeDtypeStruct((128, D), BF16)] *...]
    unnamed x2 -> x0, local copies, waits for them, and re-layouts: 4.57 us -> none
    pallas_call x0 -> x1, Pallas kernels: none -> 4.01 us  [shards(): pl.pallas_call(weigh, out_shape=[jax.ShapeDtypeStruct((128, D), BF16)] *...]
where the time goes in v2:
time: 175 us
  Pallas kernels  174 us (99%)
    pallas_call x1, Pallas kernels, shards(): pl.pallas_call(kernel, out_shape=[jax.ShapeDtypeStruct((128, D), BF16)] *...  170 us
    pallas_call x1, Pallas kernels, shards(): pl.pallas_call(weigh, out_shape=[jax.ShapeDtypeStruct((128, D), BF16)] *...  4.01 us

profile of v2, /device:TPU:1, one launch (start us, length us, event | category | flops | bytes accessed | tf_op | source)
XLA Modules:
  0.0 175.1 jit_solution(10453185716051405043)
XLA Ops:
  1.3 169.8 %shard_map.113 = (bf16[128,4096]{1,0:T(8,128)(2,1)}, bf16[128,4096]{1,0:T(8,128)(2,1)}) custom-call(s32[1,128]{1,0:T(1,128)} %bitcast.2, s32[1]{0:T(128)S(6)} %copy.12.sign_offset, s32[768,1]{1,0:T(8,128)} %constant.6.clone.swap, s32[96,4]{1,0:T(8,128)} %constant.7.clone.slots_col, s32[4,96]{1,0:T(4,128)} %constant.8.clone.slots_row, ...), custom_call_target="tpu_custom_call" | custom-call | tf_op jit(solution)/shard_map/pallas_call | solution.py:604
  171.1 4.0 %shard_map.114 = (bf16[128,4096]{1,0:T(8,128)(2,1)}, bf16[128,4096]{1,0:T(8,128)(2,1)}) custom-call(f32[1,128]{1,0:T(1,128)} %bitcast.3, bf16[128,4096]{1,0:T(8,128)(2,1)} %get-tuple-element.4.plus, bf16[128,4096]{1,0:T(8,128)(2,1)} %get-tuple-element.5.minus), custom_call_target="tpu_custom_call" | custom-call | tf_op jit(solution)/shard_map/pallas_call | solution.py:669

commit v3 on v2

--- a/solution.py
+++ b/solution.py
@@ -151,7 +151,7 @@
     def to_tokens(key_col, e):
         return one_hot(key_col == slot_keys(*[slots_row[i : i + 1, :] for i in range(4)], e))
 
-    perm[...] = one_hot(lax.broadcasted_iota(I32, (768, 768), 1) == swap[...])
+    perm[...] = one_hot(lax.broadcasted_iota(I32, (256, 256), 1) == swap[...])
 
     def swapped(value):
         return jnp.dot(perm[...], value, preferred_element_type=F32).astype(BF16)
@@ -162,11 +162,8 @@
                 [
                     jnp.concatenate(
                         [
-                            source[
-                                first + half * HALF : first + (half + 1) * HALF,
-                                c * 128 : (c + 1) * 128,
-                            ]
-                            for half in range(2)
+                            source[first + k * 16 : first + (k + 1) * 16, c * 128 : (c + 1) * 128]
+                            for k in range(2 * CAP)
                         ],
                         axis=1,
                     )
@@ -175,17 +172,36 @@
                 axis=0,
             )
         )
-        for half in range(2):
-            target[half * 768 : (half + 1) * 768, :] = laid[:, half * 128 : (half + 1) * 128]
+        for k in range(2 * CAP):
+            for p in range(16):
+                to = (k % 2 * 16 + p) * MSG + k // 2 * 16
+                target[to : to + 16, :] = laid[p * 16 : (p + 1) * 16, k * 128 : (k + 1) * 128]
 
     def unpack(source, target, first, left):
-        laid = swapped(jnp.concatenate([source[0:768, :], source[768:1536, :]], axis=1))
-        for half in range(2):
+        laid = swapped(
+            jnp.concatenate(
+                [
+                    jnp.concatenate(
+                        [
+                            source[
+                                (k % 2 * 16 + p) * MSG + k // 2 * 16 : (k % 2 * 16 + p) * MSG
+                                + (k // 2 + 1) * 16,
+                                :,
+                            ]
+                            for k in range(2 * CAP)
+                        ],
+                        axis=1,
+                    )
+                    for p in range(16)
+                ],
+                axis=0,
+            )
+        )
+        for k in range(2 * CAP):
             for c in range(16):
                 target[
-                    first + half * HALF : first + (half + 1) * HALF,
-                    left + c * 128 : left + (c + 1) * 128,
-                ] = laid[c * HALF : (c + 1) * HALF, half * 128 : (half + 1) * 128]
+                    first + k * 16 : first + (k + 1) * 16, left + c * 128 : left + (c + 1) * 128
+                ] = laid[c * 16 : (c + 1) * 16, k * 128 : (k + 1) * 128]
 
     def exchange(source, target, send_sem, recv_sem, sign):
         @pl.loop(1, PEERS)
@@ -399,12 +415,10 @@
         )
 
     def multiply(e, s):
-        acc[...] = jnp.zeros_like(acc)
-
-        @pl.loop(0, 8)
+        @pl.loop(0, 3)
         def _(k):
-            at = pl.ds(pl.multiple_of(k * 512, 512), 512)
-            acc[...] += jnp.dot(rows[e, :, at], wide[s, at, :], preferred_element_type=F32)
+            cols = pl.ds(pl.multiple_of(k * 256, 256), 256)
+            acc[:, cols] = jnp.dot(rows[e, :, :], wide[s, :, cols], preferred_element_type=F32)
 
         @pl.loop(0, 8)
         def _(i):
@@ -546,9 +560,7 @@
     ring_s(0, 1)[1]()
     move_wide(1, 96, 128)
     loads[2].wait()
-    move_down(1, 0, 48)
-    finish_s(0, 0)
-    move_down(1, 48, 96)
+    move_down(1, 0, 96)
     gathered(1)
     for e in range(2):
         for slot in range(4):
@@ -560,8 +572,9 @@
     pl.semaphore_wait(free_sem, PEERS - 1)
     multiply(1, 0)
     multiply(1, 1)
+    finish_s(0, 0)
+    ring_s(1, 0)[1]()
     finish_s(0, 1)
-    ring_s(1, 0)[1]()
     ring_s(1, 1)[1]()
     collect_t(0)
     finish_s(1, 0)
@@ -593,11 +606,11 @@
 
 
 def shards(tokens, expert_ids, gate_probs, gate_weight, up_weight, down_weight, sign_offset):
-    at = np.arange(768)
-    swap = (at % 48 // 3 * 48 + at // 48 * 3 + at % 3).astype(np.int32).reshape(768, 1)
+    at = np.arange(256)
+    swap = (at % 16 * 16 + at // 16).astype(np.int32).reshape(256, 1)
     slot = np.arange(ROWS)
-    peer = slot // CAP
-    slots = np.stack([peer // 8, peer // 2 % 4, peer % 2, slot % CAP], axis=1).astype(np.int32)
+    peer = slot % PEERS
+    slots = np.stack([peer // 8, peer // 2 % 4, peer % 2, slot // PEERS], axis=1).astype(np.int32)
     vmem, hbm = pl.BlockSpec(memory_space=pltpu.VMEM), pl.BlockSpec(memory_space=pl.ANY)
     smem = pl.BlockSpec(memory_space=pltpu.SMEM)
     dma = pltpu.SemaphoreType.DMA
@@ -626,7 +639,7 @@
             pltpu.VMEM((2, 2, 128, WIDTH), BF16),
             pltpu.VMEM((4 * ROWS, 2 * Q), F32),
             pltpu.VMEM((4 * ROWS, Q), BF16),
-            pltpu.VMEM((768, 768), BF16),
+            pltpu.VMEM((256, 256), BF16),
             dma((3,)),
             dma((3,)),
             dma((3,)),
@@ -665,13 +678,11 @@
         up_weight,
         down_weight,
     )
-    block = pl.BlockSpec((128, 1024), lambda i: (0, i))
     return pl.pallas_call(
         weigh,
         out_shape=[jax.ShapeDtypeStruct((128, D), BF16)] * 2,
-        grid=(4,),
-        in_specs=[pl.BlockSpec((1, 128), lambda i: (0, 0)), block, block],
-        out_specs=[block, block],
+        in_specs=[vmem] * 3,
+        out_specs=[vmem] * 2,
     )(gate_probs.reshape(1, 128), plus, minus)
 
 

time: 175 us -> 161 us (0.920)
  Pallas kernels: 174 us -> 160 us
    pallas_call x1, Pallas kernels: 170 us -> 156 us  [shards(): pl.pallas_call(kernel, out_shape=[jax.ShapeDtypeStruct((128, D), BF16)] *...]
where the time goes in v3:
time: 161 us
  Pallas kernels  160 us (99%)
    pallas_call x1, Pallas kernels, shards(): pl.pallas_call(kernel, out_shape=[jax.ShapeDtypeStruct((128, D), BF16)] *...  156 us
    pallas_call x1, Pallas kernels, shards(): pl.pallas_call(weigh, out_shape=[jax.ShapeDtypeStruct((128, D), BF16)] *...  3.27 us

profile of v3, /device:TPU:1, one launch (start us, length us, event | category | flops | bytes accessed | tf_op | source)
XLA Modules:
  0.0 161.0 jit_solution(5004129378501174077)
XLA Ops:
  1.3 156.4 %shard_map.113 = (bf16[128,4096]{1,0:T(8,128)(2,1)}, bf16[128,4096]{1,0:T(8,128)(2,1)}) custom-call(s32[1,128]{1,0:T(1,128)} %bitcast.2, s32[1]{0:T(128)S(6)} %copy.12.sign_offset, s32[256,1]{1,0:T(8,128)} %constant.6.clone.swap, s32[96,4]{1,0:T(8,128)} %constant.7.clone.slots_col, s32[4,96]{1,0:T(4,128)} %constant.8.clone.slots_row, ...), custom_call_target="tpu_custom_call" | custom-call | tf_op jit(solution)/shard_map/pallas_call | solution.py:617
  157.7 3.3 %shard_map.114 = (bf16[128,4096]{1,0:T(8,128)(2,1)}, bf16[128,4096]{1,0:T(8,128)(2,1)}) custom-call(f32[1,128]{1,0:T(1,128)} %bitcast.3, bf16[128,4096]{1,0:T(8,128)(2,1)} %get-tuple-element.4.plus, bf16[128,4096]{1,0:T(8,128)(2,1)} %get-tuple-element.5.minus), custom_call_target="tpu_custom_call" | custom-call | tf_op jit(solution)/shard_map/pallas_call | solution.py:681

commit v4 on v3

--- a/solution.py
+++ b/solution.py
@@ -511,6 +511,7 @@
 
     dispatch_t(0, 0)
     dispatch_s(0)
+    dispatch_s(1)
     dispatch_t(1, 0)
     loads[0].wait()
     loads[1].wait()
@@ -525,16 +526,15 @@
     move_wide(0, 56, 88)
     tokens_there(3)
     dispatch_t(0, 3)
-    dispatch_s(1)
     for slot in (1, 2, 3):
         dispatch_t(1, slot)
     move_wide(0, 88, 128)
     pass_on(0)
+    arrive_s(1)
+    gather(1)
     loads[2].wait()
     move_down(0, 0, 48)
     arrive_t(0, 0)
-    arrive_s(1)
-    gather(1)
     move_down(0, 48, 96)
     for slot in (1, 2, 3):
         arrive_t(0, slot)

time: 161 us -> 156 us (0.969)
  Pallas kernels: 160 us -> 154 us
    pallas_call x1, Pallas kernels: 156 us -> 151 us  [shards(): pl.pallas_call(kernel, out_shape=[jax.ShapeDtypeStruct((128, D), BF16)] *...]
where the time goes in v4:
time: 156 us
  Pallas kernels  154 us (99%)
    pallas_call x1, Pallas kernels, shards(): pl.pallas_call(kernel, out_shape=[jax.ShapeDtypeStruct((128, D), BF16)] *...  151 us
    pallas_call x1, Pallas kernels, shards(): pl.pallas_call(weigh, out_shape=[jax.ShapeDtypeStruct((128, D), BF16)] *...  3.27 us

profile of v4, /device:TPU:1, one launch (start us, length us, event | category | flops | bytes accessed | tf_op | source)
XLA Modules:
  0.0 155.6 jit_solution(10454038181327013647)
XLA Ops:
  1.3 151.1 %shard_map.113 = (bf16[128,4096]{1,0:T(8,128)(2,1)}, bf16[128,4096]{1,0:T(8,128)(2,1)}) custom-call(s32[1,128]{1,0:T(1,128)} %bitcast.2, s32[1]{0:T(128)S(6)} %copy.12.sign_offset, s32[256,1]{1,0:T(8,128)} %constant.6.clone.swap, s32[96,4]{1,0:T(8,128)} %constant.7.clone.slots_col, s32[4,96]{1,0:T(4,128)} %constant.8.clone.slots_row, ...), custom_call_target="tpu_custom_call" | custom-call | tf_op jit(solution)/shard_map/pallas_call | solution.py:617
  152.3 3.3 %shard_map.114 = (bf16[128,4096]{1,0:T(8,128)(2,1)}, bf16[128,4096]{1,0:T(8,128)(2,1)}) custom-call(f32[1,128]{1,0:T(1,128)} %bitcast.3, bf16[128,4096]{1,0:T(8,128)(2,1)} %get-tuple-element.4.plus, bf16[128,4096]{1,0:T(8,128)(2,1)} %get-tuple-element.5.minus), custom_call_target="tpu_custom_call" | custom-call | tf_op jit(solution)/shard_map/pallas_call | solution.py:681
